TPU v7x, 32 devices: a whole 2x2x4 slice. The times are simulated.
32 devices in a mesh: dp: 2 (over x), cent: 16 (over z, y, core).
Axes of the slice: x: 2, y: 2, z: 4, core: 2. Of those that a mesh axis runs over, the one named last changes fastest.
Arguments:
- vectors: bfloat16 [512, 1024], P(('dp', 'cent')), may hold values from -16 to 16
- centroids: bfloat16 [65536, 1024], P('cent'), may hold values from -0.1125 to 0.1125
Outputs:
- new_centroids: bfloat16 [65536, 1024], P('cent', 'dp')
- loads: float32 [65536], P('cent')
All inputs are finite; a program needn't handle non-finite values.
Results may differ from a plain program's by a relative error of at most 0.0075.
Values may be sent and summed in bfloat16 or wider, within the bound.
A program may use at most 128 MiB of HBM per device.

v0:
```python
import jax
import jax.numpy as jnp
from jax import lax
from jax.sharding import PartitionSpec as P

softness_scale = 0.1


def on_device(vectors, centroids):
    dp = lax.axis_size("dp")
    cent = lax.axis_size("cent")
    total_rows = vectors.shape[0] * dp * cent
    mass_scale = centroids.shape[0] * cent / total_rows
    rows = lax.all_gather(vectors, ("dp", "cent"), axis=0, tiled=True)
    scores = (
        lax.dot_general(
            centroids, rows, (((1,), (1,)), ((), ())), preferred_element_type=jnp.float32
        )
        / softness_scale
    )
    local_peak = jnp.max(scores, axis=0)
    exponent = jnp.exp(scores - local_peak[None, :])
    local_sum = jnp.sum(exponent, axis=0)
    stats = lax.all_gather(jnp.stack([local_peak, local_sum]), "cent", axis=0)
    highest = jnp.max(stats[:, 0], axis=0)
    summed = jnp.sum(stats[:, 1] * jnp.exp(stats[:, 0] - highest[None, :]), axis=0)
    rescale = jnp.exp(local_peak - highest) / summed
    probability = exponent * rescale[None, :]
    weights = probability.astype(jnp.bfloat16)
    loads = jnp.sum(probability, axis=1) * mass_scale
    sums = lax.dot_general(
        weights, rows, (((1,), (0,)), ((), ())), preferred_element_type=jnp.float32
    )
    shifted = centroids.astype(jnp.float32) + sums * mass_scale
    factor = lax.rsqrt(jnp.mean(shifted * shifted, axis=1, keepdims=True) + 1e-06)
    columns = centroids.shape[1] // dp
    own = lax.dynamic_slice_in_dim(shifted, lax.axis_index("dp") * columns, columns, 1)
    return ((own * factor).astype(jnp.bfloat16), loads)


def solution(mesh):
    placed = (P(("dp", "cent"), None), P("cent", None))
    return jax.shard_map(
        on_device,
        mesh=mesh,
        in_specs=placed,
        out_specs=(P("cent", "dp"), P("cent")),
        check_vma=False,
    )
```

profile of v0, /device:TPU:0, one launch (start us, length us, event | category | flops | bytes accessed | tf_op | source)
XLA Modules:
  0.0 130.6 jit_solution(8532630208074017856)
XLA Ops:
  7.2 0.0 all-gather.4.cloned.1.call-start
  7.2 0.7 all-gather.4.cloned.1.call-update
  7.9 11.3 %copy.7 = bf16[4096,1024]{0,1:T(8,128)(2,1)} copy(bf16[4096,1024]{1,0:T(8,128)(2,1)} %param.3) | data formatting | bytes 16777216 | tf_op args[1]
  19.2 48.2 %all-gather.4.cloned.1.call-done = bf16[512,1024]{1,0:T(8,128)(2,1)} async-done(((bf16[16,1024]{1,0:T(8,128)(2,1)}), bf16[512,1024]{1,0:T(8,128)(2,1)}) %all-gather.4.cloned.1.call-update) | async-done | bytes 1048592 | tf_op jit(solution)/shard_map/all_gather | solution.py:14
  67.3 7.4 %multiply_reduce_fusion.2 = (f32[512]{0:T(512)S(1)}, f32[4096,512]{1,0:T(8,128)S(1)}) fusion(bf16[4096,1024]{1,0:T(8,128)(2,1)} %param.3, bf16[512,1024]{1,0:T(8,128)(2,1)} %all-gather.4.cloned.1.call-done), kind=kOutput, calls=%fused_computation.6 | convolution fusion | flops 4299161088 | bytes 17827840 | tf_op jit(solution)/shard_map/dot_general | solution.py:16
  74.8 0.0 copy-start
  74.8 1.5 %fusion = f32[512]{0:T(512)S(1)} fusion(f32[4096,512]{1,0:T(8,128)S(1)} %get-tuple-element.10, f32[512]{0:T(512)S(1)} %get-tuple-element.9), kind=kLoop, calls=%fused_computation.7 | loop fusion | flops 6290944 | bytes 8392704 | tf_op jit(solution)/shard_map/reduce_sum | solution.py:23
  76.2 20.4 %all-gather.1 = f32[16,2,512]{2,1,0:T(2,128)S(1)} all-gather(f32[1,2,512]{2,1,0:T(2,128)S(1)} %maximum_bitcast_fusion), channel_id=2, replica_groups=mesh['dp'=2,'cent'=16] {'cent'}, dimensions={0}, use_global_device_ids=true | all-gather | bytes 69632 | tf_op jit(solution)/shard_map/all_gather | solution.py:24
  96.7 0.1 slice_reduce_fusion
  96.8 1.7 %multiply_reduce_fusion.1 = f32[4096]{0:T(1024)S(1)} fusion(f32[4096,512]{1,0:T(8,128)S(1)} %get-tuple-element.10, f32[512]{0:T(512)S(1)} %exponential_divide_fusion, f32[512]{0:T(512)S(1)} %get-tuple-element.9), kind=kLoop, calls=%fused_computation.4 | loop fusion | flops 8384512 | bytes 8409088 | tf_op jit(solution)/shard_map/reduce_sum | solution.py:30
  98.5 0.0 copy-done
  98.5 11.9 %multiply_reduce_fusion = (f32[4096]{0:T(1024)S(1)}, f32[4096,1024]{0,1:T(8,128)}) fusion(bf16[512,1024]{1,0:T(8,128)(2,1)S(1)} %copy-done, f32[4096,512]{1,0:T(8,128)S(1)} %get-tuple-element.10, f32[512]{0:T(512)S(1)} %exponential_divide_fusion, f32[512]{0:T(512)S(1)} %get-tuple-element.9, bf16[4096,1024]{0,1:T(8,128)(2,1)} %copy.7), kind=kOutput, calls=%fused_computation | convolution fusion | flops 4324323328 | bytes 34623488 | tf_op jit(solution)/shard_map/dot_general | solution.py:31
  110.5 6.3 %multiply_convert_fusion = bf16[4096,512]{0,1:T(8,128)(2,1)} fusion(f32[4096,1024]{0,1:T(8,128)} %get-tuple-element.12, s32[]{:T(128)S(6)} %select_n.3, f32[4096]{0:T(1024)S(1)} %add_rsqrt_fusion), kind=kLoop, calls=%fused_computation.2 | loop fusion | flops 4194304 | bytes 12599300 | tf_op jit(solution)/shard_map/convert_element_type | solution.py:38
  116.7 6.4 %copy.9 = bf16[4096,512]{1,0:T(8,128)(2,1)} copy(bf16[4096,512]{0,1:T(8,128)(2,1)} %multiply_convert_fusion) | data formatting | bytes 8388608
  123.1 0.6 broadcast_multiply_fusion
  (4 shorter events, 0.1 us)
Async XLA Ops:
  7.2 60.2 %all-gather.4.cloned.1.call-start = ((), (), s32[]{:S(2)}) async-start(), calls=%async_computation | async-start | bytes 1081344 | tf_op jit(solution)/shard_map/all_gather | solution.py:14
  74.8 23.8 %copy-start = (bf16[512,1024]{1,0:T(8,128)(2,1)S(1)}, bf16[512,1024]{1,0:T(8,128)(2,1)}, u32[]{:S(2)}) copy-start(bf16[512,1024]{1,0:T(8,128)(2,1)} %all-gather.4.cloned.1.call-done) | copy-start | bytes 3145732
Sparse Core Ops, SparseCore 0:
  10.9 56.4 all-gather.3
where the time goes:
time: 131 us
  waiting for transfers between devices  48.8 us (37%)
  blocking collectives  20.4 us (16%)
  matrix products  19.3 us (15%)
  local copies, waits for them, and re-layouts  17.7 us (14%)
  between operations  14.1 us (11%)
  other arithmetic  10.2 us (8%)
    all_gather x1, waiting for transfers between devices, on_device(): rows = lax.all_gather(vectors, ('dp', 'cent'), axis=0, tiled=True)  48.2 us
    all_gather x1, blocking collectives, on_device(): stats = lax.all_gather(jnp.stack([local_peak, local_sum]), 'cent', axis=0)  20.4 us
    unnamed x4, local copies, waits for them, and re-layouts  17.7 us
    dot_general x1, matrix products, on_device(): lax.dot_general(weights, rows, (((1,), (0,)), ((), ())), preferred_elemen...  11.9 us
    dot_general x1, matrix products, on_device(): lax.dot_general(centroids, rows, (((1,), (1,)), ((), ())), preferred_elem...  7.43 us
    convert_element_type x1, other arithmetic, on_device(): return ((own * factor).astype(jnp.bfloat16), loads)  6.29 us
  transfers between devices with their start and end apart: 1, of which 1 were waited for; matrix products, arithmetic and copies ran while one was open for 9% of the time, Pallas kernels for 0%

commit v1 on v0

--- a/solution.py
+++ b/solution.py
@@ -6,12 +6,35 @@
 softness_scale = 0.1
 
 
+def attach_columns_on_mesh(in_array, ndim_at):
+    local_out = list(in_array.shape[1:])
+    local_out[ndim_at] *= in_array.shape[0]
+    return jnp.moveaxis(in_array, 0, ndim_at).reshape(local_out)
+
+
+def form_rates(patch, a_name):
+    b_now = lax.axis_size(a_name)
+    raw_out = lax.axis_index(a_name)
+    tmp, y2 = (b_now, raw_out)
+    z2, y = (patch[None], 1)
+    while y < tmp:
+        r2 = tuple(((it, it ^ y) for it in range(tmp)))
+        carry_out = lax.ppermute(z2, a_name, r2)
+        formed = y2 & y == 0
+        passed = jnp.where(formed, z2, carry_out)
+        d_next = jnp.where(formed, carry_out, z2)
+        z2 = jnp.concatenate([passed, d_next])
+        y *= 2
+    return z2
+
+
 def on_device(vectors, centroids):
     dp = lax.axis_size("dp")
     cent = lax.axis_size("cent")
     total_rows = vectors.shape[0] * dp * cent
     mass_scale = centroids.shape[0] * cent / total_rows
-    rows = lax.all_gather(vectors, ("dp", "cent"), axis=0, tiled=True)
+    parts_out = form_rates(vectors, ("dp", "cent"))
+    rows = attach_columns_on_mesh(parts_out, 0)
     scores = (
         lax.dot_general(
             centroids, rows, (((1,), (1,)), ((), ())), preferred_element_type=jnp.float32

time: 131 us -> 99.2 us (0.76)
  waiting for transfers between devices: 48.8 us -> 18 us
  between operations: 14.1 us -> 0.71 us
  starting transfers between devices: 0.04 us -> 9.22 us
  other arithmetic: 10.2 us -> 13.1 us
    all_gather x1 -> x0, waiting for transfers between devices: 48.2 us -> none  [on_device(): rows = lax.all_gather(vectors, ('dp', 'cent'), axis=0, tiled=True)]
    ppermute x0 -> x5, waiting for transfers between devices: none -> 18 us  [form_rates(): carry_out = lax.ppermute(z2, a_name, r2)]
    ppermute x0 -> x5, starting transfers between devices: none -> 9.22 us  [form_rates(): carry_out = lax.ppermute(z2, a_name, r2)]
    unnamed x4 -> x8, local copies, waits for them, and re-layouts: 17.7 us -> 18.2 us
  transfers between devices with their start and end apart: 1 -> 5, of which waited for: 1 -> 5; matrix products, arithmetic and copies ran while one was open for 9% -> 12% of each run, Pallas kernels for 0% -> 0%
where the time goes in v1:
time: 99.2 us; the launch traced here: 98.6 us
  blocking collectives  21.3 us (21%)
  local copies, waits for them, and re-layouts  18.2 us (18%)
  waiting for transfers between devices  18 us (18%)
  matrix products  18 us (18%)
  other arithmetic  13.1 us (13%)
  starting transfers between devices  9.22 us (9%)
    all_gather x1, blocking collectives, on_device(): stats = lax.all_gather(jnp.stack([local_peak, local_sum]), 'cent', axis=0)  21.3 us
    unnamed x8, local copies, waits for them, and re-layouts  18.2 us
    ppermute x5, waiting for transfers between devices, form_rates(): carry_out = lax.ppermute(z2, a_name, r2)  18 us
    dot_general x1, matrix products, on_device(): lax.dot_general(weights, rows, (((1,), (0,)), ((), ())), preferred_elemen...  10.8 us
    ppermute x5, starting transfers between devices, form_rates(): carry_out = lax.ppermute(z2, a_name, r2)  9.22 us
    dot_general x1, matrix products, on_device(): lax.dot_general(centroids, rows, (((1,), (1,)), ((), ())), preferred_elem...  7.13 us
    convert_element_type x1, other arithmetic, on_device(): return ((own * factor).astype(jnp.bfloat16), loads)  6.31 us
    reduce_sum x1, other arithmetic, on_device(): loads = jnp.sum(probability, axis=1) * mass_scale  2.76 us
  transfers between devices with their start and end apart: 5, of which 5 were waited for; matrix products, arithmetic and copies ran while one was open for 12% of the time, Pallas kernels for 0%

profile of v1, /device:TPU:0, one launch (start us, length us, event | category | flops | bytes accessed | tf_op | source)
XLA Modules:
  0.0 98.6 jit_solution(1732982555747620416)
XLA Ops:
  0.6 0.5 collective-permute-start
  1.1 1.1 %collective-permute-done = bf16[1,16,1024]{2,1,0:T(8,128)(2,1)S(1)} collective-permute-done((bf16[1,16,1024]{2,1,0:T(8,128)(2,1)}, bf16[1,16,1024]{2,1,0:T(8,128)(2,1)S(1)}, u32[]{:S(2)}, u32[]{:S(2)}) %collective-permute-start) | collective-permute-done | bytes 32800 | tf_op jit(solution)/shard_map/ppermute | solution.py:22
  2.2 0.8 broadcast_select_fusion.9
  3.0 2.9 %collective-permute-start.1 = (bf16[2,16,1024]{2,1,0:T(8,128)(2,1)S(1)}, bf16[2,16,1024]{2,1,0:T(8,128)(2,1)S(1)}, u32[]{:S(2)}, u32[]{:S(2)}) collective-permute-start(bf16[2,16,1024]{2,1,0:T(8,128)(2,1)S(1)} %pad_maximum_fusion.4), channel_id=1, source_target_pairs={{0,2},{1,3},{2,0},{3,1},{4,6},{5,7},{6,4},{7,5},{8,10},{9,11},{10,... | collective-permute-start | bytes 196616 | tf_op jit(solution)/shard_map/ppermute | solution.py:22
  5.9 2.4 %collective-permute-done.1 = bf16[2,16,1024]{2,1,0:T(8,128)(2,1)S(1)} collective-permute-done((bf16[2,16,1024]{2,1,0:T(8,128)(2,1)S(1)}, bf16[2,16,1024]{2,1,0:T(8,128)(2,1)S(1)}, u32[]{:S(2)}, u32[]{:S(2)}) %collective-permute-start.1) | collective-permute-done | bytes 65568 | tf_op jit(solution)/shard_map/ppermute | solution.py:22
  8.4 2.0 %collective-permute-start.2 = (bf16[4,16,1024]{2,1,0:T(8,128)(2,1)S(1)}, bf16[4,16,1024]{2,1,0:T(8,128)(2,1)S(1)}, u32[]{:S(2)}, u32[]{:S(2)}) collective-permute-start(bf16[4,16,1024]{2,1,0:T(8,128)(2,1)S(1)} %pad_maximum_fusion.3), channel_id=1, source_target_pairs={{0,4},{1,5},{2,6},{3,7},{4,0},{5,1},{6,2},{7,3},{8,12},{9,13},{10,... | collective-permute-start | bytes 393224 | tf_op jit(solution)/shard_map/ppermute | solution.py:22
  10.4 3.1 %collective-permute-done.2 = bf16[4,16,1024]{2,1,0:T(8,128)(2,1)S(1)} collective-permute-done((bf16[4,16,1024]{2,1,0:T(8,128)(2,1)S(1)}, bf16[4,16,1024]{2,1,0:T(8,128)(2,1)S(1)}, u32[]{:S(2)}, u32[]{:S(2)}) %collective-permute-start.2) | collective-permute-done | bytes 131104 | tf_op jit(solution)/shard_map/ppermute | solution.py:22
  13.6 2.9 %collective-permute-start.3 = (bf16[8,16,1024]{2,1,0:T(8,128)(2,1)S(1)}, bf16[8,16,1024]{2,1,0:T(8,128)(2,1)S(1)}, u32[]{:S(2)}, u32[]{:S(2)}) collective-permute-start(bf16[8,16,1024]{2,1,0:T(8,128)(2,1)S(1)} %pad_maximum_fusion.2), channel_id=1, source_target_pairs={{0,8},{1,9},{2,10},{3,11},{4,12},{5,13},{6,14},{7,15},{8,0},{9,1},... | collective-permute-start | bytes 786440 | tf_op jit(solution)/shard_map/ppermute | solution.py:22
  16.5 10.6 %collective-permute-done.3 = bf16[8,16,1024]{2,1,0:T(8,128)(2,1)S(1)} collective-permute-done((bf16[8,16,1024]{2,1,0:T(8,128)(2,1)S(1)}, bf16[8,16,1024]{2,1,0:T(8,128)(2,1)S(1)}, u32[]{:S(2)}, u32[]{:S(2)}) %collective-permute-start.3) | collective-permute-done | bytes 262176 | tf_op jit(solution)/shard_map/ppermute | solution.py:22
  27.2 0.9 collective-permute-start.4
  28.1 11.8 %copy.7 = bf16[4096,1024]{0,1:T(8,128)(2,1)} copy(bf16[4096,1024]{1,0:T(8,128)(2,1)} %param.3) | data formatting | bytes 16777216 | tf_op args[1]
  39.9 0.8 collective-permute-done.4
  40.7 0.1 broadcast_select_fusion.1
  40.8 0.1 pad_maximum_fusion
  40.9 7.1 %multiply_reduce_fusion.2 = (f32[512]{0:T(512)S(1)}, f32[512,4096]{1,0:T(8,128)S(1)}) fusion(bf16[512,1024]{1,0:T(8,128)(2,1)S(1)} %bitcast.25, bf16[4096,1024]{1,0:T(8,128)(2,1)} %param.3), kind=kOutput, calls=%fused_computation.6 | convolution fusion | flops 4299161088 | bytes 17827840 | tf_op jit(solution)/shard_map/dot_general | solution.py:39
  48.0 0.0 slice-start
  48.0 1.5 %fusion = f32[512]{0:T(512)S(1)} fusion(f32[512,4096]{1,0:T(8,128)S(1)} %get-tuple-element.20, f32[512]{0:T(512)S(1)} %get-tuple-element.19), kind=kLoop, calls=%fused_computation.7 | loop fusion | flops 6290944 | bytes 8392704 | tf_op jit(solution)/shard_map/reduce_sum | solution.py:46
  49.5 21.3 %all-gather.1 = f32[16,2,512]{2,1,0:T(2,128)S(1)} all-gather(f32[1,2,512]{2,1,0:T(2,128)S(1)} %maximum_bitcast_fusion), channel_id=2, replica_groups=mesh['dp'=2,'cent'=16] {'cent'}, dimensions={0}, use_global_device_ids=true | all-gather | bytes 69632 | tf_op jit(solution)/shard_map/all_gather | solution.py:47
  70.8 0.0 slice-start.1
  70.8 0.1 slice_reduce_fusion
  70.9 2.8 %multiply_reduce_fusion.1 = f32[4096]{0:T(1024)} fusion(f32[512,4096]{1,0:T(8,128)S(1)} %get-tuple-element.20, f32[512]{0:T(512)S(1)} %exponential_divide_fusion, f32[512]{0:T(512)S(1)} %get-tuple-element.19), kind=kLoop, calls=%fused_computation.4 | loop fusion | flops 8384512 | bytes 8409088 | tf_op jit(solution)/shard_map/reduce_sum | solution.py:53
  73.7 0.0 slice-done
  73.7 0.0 slice-done.1
  73.7 10.8 %multiply_reduce_fusion = (f32[4096]{0:T(1024)}, f32[4096,1024]{0,1:T(8,128)}) fusion(bf16[512,1024]{1,0:T(8,128)(2,1)S(1)} %bitcast.26, f32[512,4096]{1,0:T(8,128)S(1)} %get-tuple-element.20, f32[512]{0:T(512)S(1)} %exponential_divide_fusion, f32[512]{0:T(512)S(1)} %get-tuple-element.19, bf16[4096,1024]{0,1:T(8,128)(2,1)S(1)} %bitcast.24), kind=kOutput, calls=%fused_computation | convolution fusion | flops 4324323328 | bytes 34623488 | tf_op jit(solution)/shard_map/dot_general | solution.py:54
  84.5 0.7 add_rsqrt_fusion
  85.3 0.0 copy-start
  85.3 6.3 %multiply_convert_fusion = bf16[4096,512]{0,1:T(8,128)(2,1)} fusion(f32[4096,1024]{0,1:T(8,128)} %get-tuple-element.22, s32[]{:T(128)S(6)} %select_n.78, f32[4096]{0:T(1024)S(1)} %add_rsqrt_fusion), kind=kLoop, calls=%fused_computation.2 | loop fusion | flops 4194304 | bytes 12599300 | tf_op jit(solution)/shard_map/convert_element_type | solution.py:61
  91.6 6.4 %copy.9 = bf16[4096,512]{1,0:T(8,128)(2,1)} copy(bf16[4096,512]{0,1:T(8,128)(2,1)} %multiply_convert_fusion) | data formatting | bytes 8388608
  98.0 0.0 copy-done
  98.0 0.6 broadcast_multiply_fusion
  (11 shorter events, 0.2 us)
Async XLA Ops:
  0.6 1.6 %collective-permute-start = (bf16[1,16,1024]{2,1,0:T(8,128)(2,1)}, bf16[1,16,1024]{2,1,0:T(8,128)(2,1)S(1)}, u32[]{:S(2)}, u32[]{:S(2)}) collective-permute-start(bf16[1,16,1024]{2,1,0:T(8,128)(2,1)} %bitcast.27), channel_id=1, source_target_pairs={{0,1},{1,0},{2,3},{3,2},{4,5},{5,4},{6,7},{7,6},{8,9},{9,8},{10,11... | collective-permute-start | bytes 98312 | tf_op jit(solution)/shard_map/ppermute | solution.py:22
  3.0 5.3 %collective-permute-start.1 = (bf16[2,16,1024]{2,1,0:T(8,128)(2,1)S(1)}, bf16[2,16,1024]{2,1,0:T(8,128)(2,1)S(1)}, u32[]{:S(2)}, u32[]{:S(2)}) collective-permute-start(bf16[2,16,1024]{2,1,0:T(8,128)(2,1)S(1)} %pad_maximum_fusion.4), channel_id=1, source_target_pairs={{0,2},{1,3},{2,0},{3,1},{4,6},{5,7},{6,4},{7,5},{8,10},{9,11},{10,... | collective-permute-start | bytes 196616 | tf_op jit(solution)/shard_map/ppermute | solution.py:22
  8.4 5.1 %collective-permute-start.2 = (bf16[4,16,1024]{2,1,0:T(8,128)(2,1)S(1)}, bf16[4,16,1024]{2,1,0:T(8,128)(2,1)S(1)}, u32[]{:S(2)}, u32[]{:S(2)}) collective-permute-start(bf16[4,16,1024]{2,1,0:T(8,128)(2,1)S(1)} %pad_maximum_fusion.3), channel_id=1, source_target_pairs={{0,4},{1,5},{2,6},{3,7},{4,0},{5,1},{6,2},{7,3},{8,12},{9,13},{10,... | collective-permute-start | bytes 393224 | tf_op jit(solution)/shard_map/ppermute | solution.py:22
  13.6 13.5 %collective-permute-start.3 = (bf16[8,16,1024]{2,1,0:T(8,128)(2,1)S(1)}, bf16[8,16,1024]{2,1,0:T(8,128)(2,1)S(1)}, u32[]{:S(2)}, u32[]{:S(2)}) collective-permute-start(bf16[8,16,1024]{2,1,0:T(8,128)(2,1)S(1)} %pad_maximum_fusion.2), channel_id=1, source_target_pairs={{0,8},{1,9},{2,10},{3,11},{4,12},{5,13},{6,14},{7,15},{8,0},{9,1},... | collective-permute-start | bytes 786440 | tf_op jit(solution)/shard_map/ppermute | solution.py:22
  27.2 13.5 %collective-permute-start.4 = (bf16[16,16,1024]{2,1,0:T(8,128)(2,1)S(1)}, bf16[16,16,1024]{2,1,0:T(8,128)(2,1)S(1)}, u32[]{:S(2)}, u32[]{:S(2)}) collective-permute-start(bf16[16,16,1024]{2,1,0:T(8,128)(2,1)S(1)} %pad_maximum_fusion.1), channel_id=1, source_target_pairs={{0,16},{1,17},{2,18},{3,19},{4,20},{5,21},{6,22},{7,23},{8,24},{9,... | collective-permute-start | bytes 1572872 | tf_op jit(solution)/shard_map/ppermute | solution.py:22
  48.0 25.7 %slice-start = ((s8[8388608]{0:T(1024)(128)(4,1)}), s8[4194304]{0:T(1024)(128)(4,1)S(1)}, s32[]{:S(2)}) async-start(s8[8388608]{0:T(1024)(128)(4,1)} %bitcast.23), calls=%async_computation | async-start | bytes 8388608
  70.8 2.9 %slice-start.1 = ((s8[8388608]{0:T(1024)(128)(4,1)}), s8[4194304]{0:T(1024)(128)(4,1)S(1)}, s32[]{:S(2)}) async-start(s8[8388608]{0:T(1024)(128)(4,1)} %bitcast.23), calls=%async_computation.1 | async-start | bytes 8388608
  85.3 12.7 %copy-start = (f32[4096]{0:T(1024)S(1)}, f32[4096]{0:T(1024)}, u32[]{:S(2)}) copy-start(f32[4096]{0:T(1024)} %multiply_reduce_fusion.1) | copy-start | bytes 49156
